TPU v7x, 128 devices: a whole 4x4x4 slice. The times are simulated.
128 devices in a mesh: ctx: 16 (over z, x_hi, core), samp: 4 (over y), tp: 2 (over x_lo).
Axes of the slice: x: 4 (x_hi: 2, x_lo: 2; x = x_hi * 2 + x_lo), y: 4, z: 4, core: 2. Of those that a mesh axis runs over, the one named last changes fastest.
Arguments:
- queries: bfloat16 [64, 256, 6144], P(('ctx', 'samp'), None, 'tp'), may hold values from -4.5 to 4.5
- out_grad: bfloat16 [64, 256, 6144], P(('ctx', 'samp'), None, 'tp'), may hold values from -12 to 12
- answer_kv: bfloat16 [64, 256, 256], P(('ctx', 'samp')), may hold values from -4.5 to 4.5
- prompt_kv: bfloat16 [4, 1024, 256], P(None, 'ctx'), may hold values from -4.5 to 4.5
- answer_prompt: int32 [64], P(('ctx', 'samp')), may hold values from 0 to 3, as said below
- answer_len: int32 [64], P(('ctx', 'samp')), may hold values from 32 to 256
Outputs:
- query_grad: float32 [64, 256, 6144], P(('ctx', 'samp'), None, 'tp')
- answer_kv_grad: float32 [64, 256, 256], P(('ctx', 'samp'))
- prompt_kv_grad: float32 [4, 1024, 256], P(None, 'ctx')
Inputs may be any that keep to these rules, and one draw needn't show every extreme that they name: `answer_prompt`: every one of the 4 prompts is continued by at least one answer.
All inputs are finite; a program needn't handle non-finite values.
Results may differ from a plain program's by a relative error of at most 0.02.
Values may be sent and summed in bfloat16 or wider, within the bound.
A program may use at most 192 MiB of HBM per device.

v0:
```python
import jax
import jax.numpy as jnp
from jax import lax
from jax.sharding import PartitionSpec as P


def sections(total_rows):
    return [(offset, min(512, total_rows - offset)) for offset in range(0, total_rows, 512)]


def body(queries, out_grad, answer_kv, prompt_kv, answer_prompt, answer_len):
    answer_count, answer_length, head_cols = queries.shape
    head_width = answer_kv.shape[2] // 2
    heads_here = head_cols // head_width
    prompt_count = prompt_kv.shape[0]
    prompt_length = prompt_kv.shape[1] * lax.axis_size("ctx")
    score_scale = head_width ** (-0.5)
    positions = jnp.arange(answer_length, dtype=jnp.int32)
    live_rows = positions[None, :] < answer_len[:, None]
    q_heads = queries.reshape(answer_count, answer_length, heads_here, head_width)
    grad_in = jnp.where(live_rows[:, :, None], out_grad, jnp.zeros_like(out_grad))
    g_heads = grad_in.reshape(answer_count, answer_length, heads_here, head_width)
    causal = positions[:, None] >= positions[None, :]
    owners = (jnp.arange(prompt_count, dtype=jnp.int32)[:, None] == answer_prompt[None, :]).astype(
        jnp.float32
    )

    def key_scores(kv_rows, mask):
        scores = (
            jnp.einsum(
                "athd,akd->athk",
                q_heads,
                kv_rows[:, :, :head_width],
                preferred_element_type=jnp.float32,
            )
            * score_scale
        )
        if mask is None:
            return scores
        return jnp.where(mask[None, :, None, :], scores, -jnp.inf)

    def gather_rows(kv_piece):
        return jnp.take(kv_piece, answer_prompt, axis=0)

    def add_stats(running, scores):
        row_top, row_total = running
        new_top = jnp.maximum(row_top, jnp.max(scores, axis=-1))
        row_total = row_total * jnp.exp(row_top - new_top) + jnp.sum(
            jnp.exp(scores - new_top[..., None]), axis=-1
        )
        return (new_top, row_total)

    start_top = jnp.full((answer_count, answer_length, heads_here), -jnp.inf, jnp.float32)
    start_total = jnp.zeros((answer_count, answer_length, heads_here), jnp.float32)
    softmax_stats = add_stats((start_top, start_total), key_scores(answer_kv, causal))
    whole_kv = lax.all_gather(prompt_kv, "ctx", axis=1, tiled=True)
    running = softmax_stats
    chosen = gather_rows(whole_kv)
    for offset, length in sections(whole_kv.shape[1]):
        running = add_stats(running, key_scores(chosen[:, offset : offset + length], None))
    softmax_stats = running

    def block_terms(kv_rows, mask):
        scores = key_scores(kv_rows, mask)
        probs = jnp.exp(scores - softmax_stats[0][..., None]) / softmax_stats[1][..., None]
        probs_b = probs.astype(jnp.bfloat16)
        dprobs = jnp.einsum(
            "athd,akd->athk",
            g_heads,
            kv_rows[:, :, head_width:],
            preferred_element_type=jnp.float32,
        )
        return (probs, probs_b, dprobs)

    def delta_terms(kv_rows, mask):
        probs, probs_b, dprobs = block_terms(kv_rows, mask)
        return jnp.sum(probs_b.astype(jnp.float32) * dprobs, axis=-1)

    row_delta = delta_terms(answer_kv, causal)
    running = row_delta
    chosen = gather_rows(whole_kv)
    for offset, length in sections(whole_kv.shape[1]):
        running = running + delta_terms(chosen[:, offset : offset + length], None)
    row_delta = running

    def grad_terms(kv_rows, mask):
        probs, probs_b, dprobs = block_terms(kv_rows, mask)
        dscores_b = (probs * (dprobs - row_delta[..., None])).astype(jnp.bfloat16)
        query_part = jnp.einsum(
            "athk,akd->athd",
            dscores_b,
            kv_rows[:, :, :head_width],
            preferred_element_type=jnp.float32,
        )
        key_grad = (
            jnp.einsum("athk,athd->akd", dscores_b, q_heads, preferred_element_type=jnp.float32)
            * score_scale
        )
        value_grad = jnp.einsum(
            "athk,athd->akd", probs_b, g_heads, preferred_element_type=jnp.float32
        )
        return (query_part, jnp.concatenate([key_grad, value_grad], axis=-1))

    query_acc, own_grad = grad_terms(answer_kv, causal)
    prompt_acc = jnp.zeros((prompt_count, prompt_length, 2 * head_width), jnp.float32)
    grad_query_acc = query_acc
    grad_prompt_acc = prompt_acc
    chosen = gather_rows(whole_kv)
    for offset, length in sections(whole_kv.shape[1]):
        query_part, kv_grad = grad_terms(chosen[:, offset : offset + length], None)
        grad_query_acc = grad_query_acc + query_part
        by_prompt = jnp.einsum("pa,akc->pkc", owners, kv_grad, precision=lax.Precision.HIGHEST)
        row_start = 0 + offset
        current = lax.dynamic_slice_in_dim(grad_prompt_acc, row_start, length, 1)
        grad_prompt_acc = lax.dynamic_update_slice_in_dim(
            grad_prompt_acc, current + by_prompt, row_start, 1
        )
    query_grad = (grad_query_acc * score_scale).reshape(answer_count, answer_length, head_cols)
    answer_kv_grad = lax.psum(own_grad, "tp")
    block_part = lax.psum_scatter(grad_prompt_acc, "ctx", scatter_dimension=1, tiled=True)
    prompt_kv_grad = lax.psum(block_part, ("samp", "tp"))
    return (query_grad, answer_kv_grad, prompt_kv_grad)


def solution(mesh):
    placed = (
        P(("ctx", "samp"), None, "tp"),
        P(("ctx", "samp"), None, "tp"),
        P(("ctx", "samp"), None, None),
        P(None, "ctx", None),
        P(("ctx", "samp")),
        P(("ctx", "samp")),
    )
    return jax.shard_map(
        body,
        mesh=mesh,
        in_specs=placed,
        out_specs=(
            P(("ctx", "samp"), None, "tp"),
            P(("ctx", "samp"), None, None),
            P(None, "ctx", None),
        ),
        check_vma=False,
    )
```

profile of v0, /device:TPU:1, one launch (start us, length us, event | category | flops | bytes accessed | tf_op | source)
XLA Modules:
  0.0 339.0 jit_solution(11725306481435914150)
XLA Ops:
  14.4 2.6 copy-done.2
  18.3 43.5 %all-gather.2.cloned.1.call-done = bf16[4,1024,256]{2,1,0:T(8,128)(2,1)} async-done(((bf16[4,64,256]{2,1,0:T(8,128)(2,1)}), bf16[4,1024,256]{2,1,0:T(8,128)(2,1)}) %all-gather.2.cloned.1.call-update) | async-done | bytes 2097168 | tf_op jit(solution)/shard_map/all_gather | solution.py:56
  66.5 6.9 %fusion.29 = f32[256,24,512]{0,2,1:T(8,128)} fusion(bf16[256,24,128]{0,2,1:T(8,128)(2,1)S(1)} %bitcast.153, bf16[1,1024,256]{2,1,0:T(8,128)(2,1)S(1)} %dynamic-slice_select_fusion), kind=kOutput, calls=%fused_computation.51 | convolution fusion | flops 805306368 | bytes 14286848 | tf_op jit(solution)/shard_map/athd,akd->athk/dot_general | solution.py:67
  73.4 4.4 %fusion.2 = (f32[256,24]{0,1:T(8,128)S(1)}, f32[256,24]{0,1:T(8,128)S(1)}) fusion(f32[512,256,24]{1,0,2:T(8,128)S(1)} %get-tuple-element.31, f32[256,24]{0,1:T(8,128)S(1)} %get-tuple-element.21, f32[256,24]{0,1:T(8,128)S(1)} %get-tuple-element.20, f32[512,256,24]{1,0,2:T(8,128)S(1)} %get-tuple-element.27), kind=kLoop, calls=%fused_computation.7 | loop fusion | flops 18862080 | bytes 25264128 | tf_op jit(solution)/shard_map/reduce_sum | solution.py:48
  77.8 2.9 fusion.17
  80.8 3.6 %fusion.14 = f32[1,512,128]{1,2,0:T(8,128)} fusion(bf16[256,24,128]{0,2,1:T(8,128)(2,1)S(1)} %bitcast.155, f32[512,256,24]{1,0,2:T(8,128)S(1)} %get-tuple-element.31, f32[256,24]{0,1:T(8,128)S(1)} %multiply_add_fusion, f32[256,24]{0,1:T(8,128)S(1)} %get-tuple-element.20), kind=kOutput, calls=%fused_computation.31 | convolution fusion | flops 817889280 | bytes 14467072 | tf_op jit(solution)/shard_map/athk,athd->akd/dot_general | solution.py:99
  84.4 4.4 %multiply_reduce_fusion.2 = (f32[256,24]{0,1:T(8,128)}, f32[256,24,256]{0,2,1:T(8,128)}) fusion(f32[256,24]{0,1:T(8,128)S(1)} %multiply_add_fusion, f32[256,24]{0,1:T(8,128)S(1)} %get-tuple-element.20, f32[256,24,256]{0,2,1:T(8,128)S(1)} %bitcast.152, pred[256,256]{0,1:T(8,128)(4,1)S(1)} %iota_compare_fusion, bf16[256,24,128]{0,2,1:T(8,128)(2,1)S(1)} %bitcast.156, ...), kind=kOutput, calls=%fused_computation.17 | convolution fusion | flops 415229952 | bytes 14360576 | tf_op jit(solution)/shard_map/athd,akd->athk/dot_general | solution.py:67
  88.7 20.0 %multiply_reduce_fusion.1 = (f32[256,24]{0,1:T(8,128)}, f32[256,24]{0,1:T(8,128)}, f32[256,24,512]{0,2,1:T(8,128)}) fusion(f32[256,24]{0,1:T(8,128)S(1)} %multiply_add_fusion, f32[256,24]{0,1:T(8,128)S(1)} %get-tuple-element.20, f32[512,256,24]{1,0,2:T(8,128)} %copy-done.1, f32[256,24,512]{0,2,1:T(8,128)} %fusion.29, f32[512,256,24]{1,0,2:T(8,128)} %copy-done, ...), kind=kOutput, calls=%fused_computation.13 | convolution fusion | flops 849334272 | bytes 52133888 | tf_op jit(solution)/shard_map/athd,akd->athk/dot_general | solution.py:67
  109.6 20.5 %multiply_convert_fusion = (bf16[256,24,512]{0,2,1:T(8,128)(2,1)S(1)}, bf16[256,24,512]{0,2,1:T(8,128)(2,1)}) fusion(f32[256,24,512]{0,2,1:T(8,128)} %fusion.29, f32[256,24]{0,1:T(8,128)S(1)} %add_add_fusion, f32[256,24]{0,1:T(8,128)S(1)} %multiply_add_fusion, f32[256,24]{0,1:T(8,128)S(1)} %get-tuple-element.20, f32[512,256,24]{1,0,2:T(8,128)} %copy-done, ...), kind=kLoop, calls=%fused_computation.10 | loop fusion | flops 37748736 | bytes 62988288 | tf_op jit(solution)/shard_map/convert_element_type | solution.py:88
  130.1 2.8 fusion.21
  132.9 2.3 copy-done.5
  135.2 2.1 fusion.23
  138.2 2.0 copy.33
  142.0 2.0 copy.38
  145.7 2.3 pad_maximum_fusion
  148.0 5.7 %multiply_convert_fusion.2 = bf16[256,24,256]{0,2,1:T(8,128)(2,1)S(1)} fusion(f32[256,24,256]{0,2,1:T(8,128)} %get-tuple-element.34, f32[256,24]{0,1:T(8,128)S(1)} %add_add_fusion, f32[256,24]{0,1:T(8,128)S(1)} %multiply_add_fusion, f32[256,24]{0,1:T(8,128)S(1)} %get-tuple-element.20, f32[256,24,256]{0,2,1:T(8,128)} %copy-done.2, ...), kind=kLoop, calls=%fused_computation.16 | loop fusion | flops 11010048 | bytes 15867904 | tf_op jit(solution)/shard_map/convert_element_type | solution.py:88
  154.9 4.9 %fusion.26 = f32[1,256,128]{1,2,0:T(8,128)S(1)} fusion(bf16[256,24,128]{0,2,1:T(8,128)(2,1)S(1)} %bitcast.158, f32[256,24,256]{0,2,1:T(8,128)} %copy-done.2, f32[256,24]{0,1:T(8,128)S(1)} %multiply_add_fusion, f32[256,24]{0,1:T(8,128)S(1)} %get-tuple-element.20, pred[256,256]{0,1:T(8,128)(4,1)S(1)} %iota_compare_fusion), kind=kOutput, calls=%fused_computation.42 | convolution fusion | flops 410517504 | bytes 8110080 | tf_op jit(solution)/shard_map/athk,athd->akd/dot_general | solution.py:99
  160.6 5.9 %fusion.31 = f32[256,24,128]{0,2,1:T(8,128)} fusion(bf16[256,24,512]{0,2,1:T(8,128)(2,1)} %get-tuple-element.23, bf16[1,1024,256]{2,1,0:T(8,128)(2,1)S(1)} %copy-done.7), kind=kOutput, calls=%fused_computation.56 | convolution fusion | flops 805306368 | bytes 9568256 | tf_op jit(solution)/shard_map/athk,akd->athd/dot_general | solution.py:89
  166.5 4.3 %fusion.36 = f32[256,24,128]{0,2,1:T(8,128)} fusion(bf16[256,24,256]{0,2,1:T(8,128)(2,1)} %copy-done.3, bf16[1,256,256]{2,1,0:T(8,128)(2,1)S(1)} %copy-done.11), kind=kOutput, calls=%fused_computation.61 | convolution fusion | flops 402653184 | bytes 6356992 | tf_op jit(solution)/shard_map/athk,akd->athd/dot_general | solution.py:89
  170.8 55.0 %reduce-scatter.2.cloned.1.call-done = f32[4,64,256]{2,1,0:T(8,128)} async-done(((f32[4,1024,256]{2,1,0:T(8,128)}), f32[4,64,256]{2,1,0:T(8,128)}) %reduce-scatter.2.cloned.1.call-update) | async-done | bytes 262160 | tf_op jit(solution)/shard_map/reduce_scatter | solution.py:120
  225.8 7.7 %add_multiply_fusion = f32[256,24,128]{0,2,1:T(8,128)} fusion(f32[256,24,128]{0,2,1:T(8,128)} %fusion.36, f32[256,24,128]{0,2,1:T(8,128)} %fusion.31, bf16[256,24,512]{0,2,1:T(8,128)(2,1)} %copy-done.4, bf16[1,1024,256]{2,1,0:T(8,128)(2,1)S(1)} %copy-done.7), kind=kOutput, calls=%fused_computation.23 | convolution fusion | flops 807665664 | bytes 15859712 | tf_op jit(solution)/shard_map/athk,akd->athd/dot_general | solution.py:89
  233.5 3.5 %copy.39 = f32[1,256,3072]{2,1,0:T(8,128)} copy(f32[1,256,3072]{1,2,0:T(8,128)} %bitcast.159) | data formatting | bytes 6291456
  237.1 21.3 %all-reduce.3.cloned.1.call-done = f32[1,256,256]{1,2,0:T(8,128)} async-done(((f32[1,256,256]{1,2,0:T(8,128)}), f32[1,256,256]{1,2,0:T(8,128)}) %all-reduce.3.cloned.1.call-update) | async-done | bytes 262160 | tf_op jit(solution)/shard_map/psum | solution.py:119
  260.2 70.6 %all-reduce.5.cloned.1.call-done = f32[4,64,256]{2,1,0:T(8,128)} async-done(((f32[4,64,256]{2,1,0:T(8,128)}), f32[4,64,256]{2,1,0:T(8,128)}) %all-reduce.5.cloned.1.call-update) | async-done | bytes 262160 | tf_op jit(solution)/shard_map/psum | solution.py:121
  (56 shorter events, 22.3 us)
Async XLA Ops:
  7.2 6.2 %copy-start.9 = (bf16[1,256,256]{2,1,0:T(8,128)(2,1)S(1)}, bf16[1,256,256]{2,1,0:T(8,128)(2,1)}, u32[]{:S(2)}) copy-start(bf16[1,256,256]{2,1,0:T(8,128)(2,1)} %param.10) | copy-start | bytes 393220
  7.2 54.6 %all-gather.2.cloned.1.call-start = ((), (), s32[]{:S(2)}) async-start(), calls=%async_computation.1 | async-start | bytes 2228224 | tf_op jit(solution)/shard_map/all_gather | solution.py:56
  7.9 217.9 %reduce-scatter.2.cloned.1.call-start = ((), (), s32[]{:S(2)}) async-start(), calls=%async_computation.3 | async-start | bytes 4456448 | tf_op jit(solution)/shard_map/reduce_scatter | solution.py:120
  14.4 2.6 copy-start.2
  62.8 3.7 %copy-start.6 = (bf16[1,1024,256]{2,1,0:T(8,128)(2,1)}, bf16[1,1024,256]{2,1,0:T(8,128)(2,1)S(1)}, u32[]{:S(2)}) copy-start(bf16[1,1024,256]{2,1,0:T(8,128)(2,1)S(1)} %dynamic-slice_select_fusion) | copy-start | bytes 1572868
  64.7 13.2 %copy-start = (f32[512,256,24]{1,0,2:T(8,128)}, f32[512,256,24]{1,0,2:T(8,128)S(1)}, u32[]{:S(2)}) copy-start(f32[512,256,24]{1,0,2:T(8,128)S(1)} %get-tuple-element.27) | copy-start | bytes 37748740
  66.5 14.2 %copy-start.1 = (f32[512,256,24]{1,0,2:T(8,128)}, f32[512,256,24]{1,0,2:T(8,128)S(1)}, u32[]{:S(2)}) copy-start(f32[512,256,24]{1,0,2:T(8,128)S(1)} %get-tuple-element.31) | copy-start | bytes 37748740
  77.8 6.5 %slice-start = ((s8[6291456]{0:T(1024)(128)(4,1)}), s8[4194304]{0:T(1024)(128)(4,1)S(1)}, s32[]{:S(2)}) async-start(s8[6291456]{0:T(1024)(128)(4,1)} %bitcast.151), calls=%async_computation.5 | async-start | bytes 8388608
  80.7 3.6 %slice-start.1 = ((s8[6291456]{0:T(1024)(128)(4,1)}), s8[2097152]{0:T(1024)(128)(4,1)S(1)}, s32[]{:S(2)}) async-start(s8[6291456]{0:T(1024)(128)(4,1)} %bitcast.151), calls=%async_computation.6 | async-start | bytes 4194304
  80.7 3.6 %copy-start.10 = (bf16[1,256,256]{2,1,0:T(8,128)(2,1)S(1)}, bf16[1,256,256]{2,1,0:T(8,128)(2,1)}, u32[]{:S(2)}) copy-start(bf16[1,256,256]{2,1,0:T(8,128)(2,1)} %param.10) | copy-start | bytes 393220
  130.0 7.3 %copy-start.4 = (bf16[256,24,512]{0,2,1:T(8,128)(2,1)}, bf16[256,24,512]{0,2,1:T(8,128)(2,1)S(1)}, u32[]{:S(2)}) copy-start(bf16[256,24,512]{0,2,1:T(8,128)(2,1)S(1)} %get-tuple-element.22) | copy-start | bytes 18874372
  130.0 5.1 %copy-start.5 = (bf16[256,24,512]{0,2,1:T(8,128)(2,1)S(1)}, bf16[256,24,512]{0,2,1:T(8,128)(2,1)}, u32[]{:S(2)}) copy-start(bf16[256,24,512]{0,2,1:T(8,128)(2,1)} %get-tuple-element.23) | copy-start | bytes 18874372
  130.0 7.3 %copy-start.8 = (f32[1,512,128]{1,2,0:T(8,128)S(1)}, f32[1,512,128]{1,2,0:T(8,128)}, u32[]{:S(2)}) copy-start(f32[1,512,128]{1,2,0:T(8,128)} %fusion.14) | copy-start | bytes 786436
  148.0 110.4 %all-reduce.3.cloned.1.call-start = ((), (), s32[]{:S(2)}) async-start(), calls=%async_computation.2 | async-start | bytes 524288 | tf_op jit(solution)/shard_map/psum | solution.py:119
  153.8 6.0 %copy-start.3 = (bf16[256,24,256]{0,2,1:T(8,128)(2,1)}, bf16[256,24,256]{0,2,1:T(8,128)(2,1)S(1)}, u32[]{:S(2)}) copy-start(bf16[256,24,256]{0,2,1:T(8,128)(2,1)S(1)} %multiply_convert_fusion.2) | copy-start | bytes 9437188
  154.9 5.6 %copy-start.7 = (bf16[1,1024,256]{2,1,0:T(8,128)(2,1)S(1)}, bf16[1,1024,256]{2,1,0:T(8,128)(2,1)}, u32[]{:S(2)}) copy-start(bf16[1,1024,256]{2,1,0:T(8,128)(2,1)} %copy-done.6) | copy-start | bytes 1572868
  159.8 6.7 %copy-start.11 = (bf16[1,256,256]{2,1,0:T(8,128)(2,1)S(1)}, bf16[1,256,256]{2,1,0:T(8,128)(2,1)}, u32[]{:S(2)}) copy-start(bf16[1,256,256]{2,1,0:T(8,128)(2,1)} %param.10) | copy-start | bytes 393220
  166.5 164.3 %all-reduce.5.cloned.1.call-start = ((), (), s32[]{:S(2)}) async-start(), calls=%async_computation.4 | async-start | bytes 524288 | tf_op jit(solution)/shard_map/psum | solution.py:121
Sparse Core Ops, SparseCore 0:
  10.5 51.2 all-gather.1
  148.1 77.6 reduce-scatter.1
  228.9 29.4 all-reduce.2
  260.7 70.0 all-reduce.4
where the time goes:
time: 344 us; the launch traced here: 339 us
  waiting for transfers between devices  191 us (56%)
  matrix products  71.3 us (21%)
  other arithmetic  42.7 us (12%)
  local copies, waits for them, and re-layouts  18.4 us (5%)
  between operations  15.4 us (4%)
    psum x1, waiting for transfers between devices, body(): prompt_kv_grad = lax.psum(block_part, ('samp', 'tp'))  70.6 us
    reduce_scatter x1, waiting for transfers between devices, body(): lax.psum_scatter(grad_prompt_acc, 'ctx', scatter_dimension=1, tiled=True)  55 us
    all_gather x1, waiting for transfers between devices, body(): whole_kv = lax.all_gather(prompt_kv, 'ctx', axis=1, tiled=True)  43.5 us
    dot_general x3, matrix products, block_terms(): jnp.einsum('athd,akd->athk', g_heads, kv_rows[:, :, head_width:], preferr...  31.3 us
    convert_element_type x2, other arithmetic, grad_terms(): dscores_b = (probs * (dprobs - row_delta[..., None])).astype(jnp.bfloat16)  26.2 us
    psum x1, waiting for transfers between devices, body(): answer_kv_grad = lax.psum(own_grad, 'tp')  21.3 us
    dot_general x3, matrix products, grad_terms(): jnp.einsum('athk,akd->athd', dscores_b, kv_rows[:, :, :head_width], prefe...  17.9 us
    unnamed x31, local copies, waits for them, and re-layouts  11.9 us
  transfers between devices with their start and end apart: 4, of which 4 were waited for; matrix products, arithmetic and copies ran while one was open for 12% of the time, Pallas kernels for 0%

commit v1 on v0

v1 whole, which is shorter than its diff:
```python
import functools

import jax
import jax.numpy as jnp
from jax import lax
from jax.experimental import pallas as pl
from jax.experimental.pallas import tpu as pltpu
from jax.sharding import PartitionSpec as P

BF = jnp.bfloat16
F32 = jnp.float32
T = 256
D = 128
PK = 1024
NK = PK + T
NP = 4
NC = 16
BL = PK // NC
NG = 8
SCALE = D**-0.5
EXP2 = SCALE * 1.4426950408889634
RC = 32
MESH = pl.DeviceIdType.MESH
VM = pl.BlockSpec(memory_space=pltpu.VMEM)
SM = pl.BlockSpec(memory_space=pltpu.SMEM)


def one_hot_tile(prompt):
    rows = lax.broadcasted_iota(jnp.int32, (8, 128), 0)
    return jnp.where(rows == prompt, 1.0, 0.0).astype(F32)


def weight_row(tile, prompt):
    row = tile[prompt : prompt + 1, :]
    return jnp.concatenate([row, row], axis=1)


def gather_kernel(ap_ref, kv_ref, out_ref, hot_ref, hot_send, send_buf, hs, hr, ds, dr):
    me = lax.axis_index("ctx")
    barrier = pltpu.get_barrier_semaphore()
    for i in range(1, NC):
        pl.semaphore_signal(
            barrier, inc=1, device_id={"ctx": lax.rem(me + i, NC)}, device_id_type=MESH
        )
    tile = one_hot_tile(ap_ref[0])
    hot_send[...] = tile
    hot_ref[me] = tile
    pl.semaphore_wait(barrier, NC - 1)

    def hot_copy(i):
        return pltpu.make_async_remote_copy(
            src_ref=hot_send,
            dst_ref=hot_ref.at[me],
            send_sem=hs.at[i],
            recv_sem=hr.at[i],
            device_id={"ctx": lax.rem(me + i, NC)},
            device_id_type=MESH,
        )

    def block_copy(i):
        return pltpu.make_async_remote_copy(
            src_ref=send_buf.at[i],
            dst_ref=out_ref.at[me],
            send_sem=ds.at[i],
            recv_sem=dr.at[i],
            device_id={"ctx": lax.rem(me + i, NC)},
            device_id_type=MESH,
        )

    for i in range(1, NC):
        hot_copy(i).start()

    def chosen(weights):
        total = kv_ref[0].astype(F32) * weight_row(weights, 0)
        for p in range(1, NP):
            total = total + kv_ref[p].astype(F32) * weight_row(weights, p)
        return total.astype(BF)

    out_ref[me] = chosen(tile)
    for i in range(1, NC):
        hot_copy(NC - i).wait_recv()
        send_buf[i] = chosen(hot_ref[lax.rem(me + i, NC)])
        block_copy(i).start()
    for i in range(1, NC):
        hot_copy(i).wait_send()
        block_copy(i).wait()


def gather(answer_prompt, prompt_kv):
    dma = pltpu.SemaphoreType.DMA((NC,))
    return pl.pallas_call(
        gather_kernel,
        out_shape=(
            jax.ShapeDtypeStruct((NC, BL, 2 * D), BF),
            jax.ShapeDtypeStruct((NC, 8, 128), F32),
        ),
        in_specs=[SM, VM],
        out_specs=(VM, VM),
        scratch_shapes=[pltpu.VMEM((8, 128), F32), pltpu.VMEM((NC, BL, 2 * D), BF), dma, dma, dma, dma],
        compiler_params=pltpu.CompilerParams(collective_id=0, has_side_effects=True),
        name="gather_prompt",
    )(answer_prompt, prompt_kv)


def head_cols(h):
    return pl.ds(pl.multiple_of(h * D, D), D)


def head_rows(h):
    return pl.ds(pl.multiple_of(h * T, T), T)


def prepare(h, q_ref, g_ref, gm, qt, gt, live):
    rows = lax.broadcasted_iota(jnp.int32, (T, D), 0)
    g = jnp.where(rows < live, g_ref[:, head_cols(h)].astype(F32), 0.0).astype(BF)
    gm[:, head_cols(h)] = g
    qt[:, head_rows(h)] = q_ref[:, head_cols(h)].T
    gt[:, head_rows(h)] = g.T


def products(h, q_ref, gm, kt, vt, s_buf, d_buf):
    s_buf[...] = jnp.dot(q_ref[:, head_cols(h)], kt[...], preferred_element_type=F32)
    d_buf[...] = jnp.dot(gm[:, head_cols(h)], vt[...], preferred_element_type=F32)


def softmax_terms(h, s_buf, d_buf, probs, dscores):
    for r in range(T // RC):
        r0 = r * RC
        width = PK + (128 if r0 < 128 else 256)
        rows = slice(r0, r0 + RC)
        out_rows = pl.ds(pl.multiple_of(h * T + r0, RC), RC)
        s = s_buf[rows, :width]
        row = lax.broadcasted_iota(jnp.int32, (RC, 128), 0) + (r0 % 128)
        col = lax.broadcasted_iota(jnp.int32, (RC, 128), 1)
        last = jnp.where(row >= col, s[:, width - 128 :], -jnp.inf)
        s = jnp.concatenate([s[:, : width - 128], last], axis=1)
        top = jnp.max(s, axis=1, keepdims=True)
        e = jnp.exp2((s - top) * EXP2)
        p = e * (1.0 / jnp.sum(e, axis=1, keepdims=True))
        probs[out_rows, :width] = p.astype(BF)
        d = d_buf[rows, :width]
        delta = jnp.sum(p * d, axis=1, keepdims=True)
        dscores[out_rows, :width] = (p * (d - delta)).astype(BF)
        if width < NK:
            probs[out_rows, width:] = jnp.zeros((RC, NK - width), BF)
            dscores[out_rows, width:] = jnp.zeros((RC, NK - width), BF)


def compute_kernel(
    heads, len_ref, q_ref, g_ref, pkv_ref, akv_ref, dq, dpkv, dakv,
    s0, s1, d0, d1, probs, dscores, qt, gt, gm, kt, vt, keys,
):
    live = len_ref[0]
    kt[:, :PK] = pkv_ref[:, :D].T
    vt[:, :PK] = pkv_ref[:, D:].T
    kt[:, PK:] = akv_ref[:, :D].T
    vt[:, PK:] = akv_ref[:, D:].T
    keys[:PK, :] = pkv_ref[:, :D]
    keys[PK:, :] = akv_ref[:, :D]

    def query_out(h):
        dq[:, head_cols(h)] = (
            jnp.dot(dscores[head_rows(h), :], keys[...], preferred_element_type=F32) * SCALE
        )

    prepare(0, q_ref, g_ref, gm, qt, gt, live)
    products(0, q_ref, gm, kt, vt, s0, d0)

    def step(h, now, later):
        after = jnp.minimum(h + 1, heads - 1)
        prepare(after, q_ref, g_ref, gm, qt, gt, live)
        products(after, q_ref, gm, kt, vt, *later)
        softmax_terms(h, *now, probs, dscores)
        query_out(h)

    def two_heads(i, carry):
        step(2 * i, (s0, d0), (s1, d1))
        step(2 * i + 1, (s1, d1), (s0, d0))
        return carry

    lax.fori_loop(0, heads // 2, two_heads, 0)
    for j in range(NK // 256):
        at = slice(j * 256, (j + 1) * 256)
        key_grad = jnp.dot(qt[...], dscores[:, at], preferred_element_type=F32) * SCALE
        value_grad = jnp.dot(gt[...], probs[:, at], preferred_element_type=F32)
        if j * 256 < PK:
            dpkv[at, :D] = key_grad.T.astype(BF)
            dpkv[at, D:] = value_grad.T.astype(BF)
        else:
            dakv[:, :D] = key_grad.T.astype(BF)
            dakv[:, D:] = value_grad.T.astype(BF)


def compute(answer_len, q, g, pkv, akv):
    heads = q.shape[1] // D
    rows = heads * T
    scratch = (
        [pltpu.VMEM((T, NK), F32)] * 4
        + [pltpu.VMEM((rows, NK), BF)] * 2
        + [pltpu.VMEM((D, rows), BF)] * 2
        + [pltpu.VMEM((T, heads * D), BF)]
        + [pltpu.VMEM((D, NK), BF)] * 2
        + [pltpu.VMEM((NK, D), BF)]
    )
    return pl.pallas_call(
        functools.partial(compute_kernel, heads),
        out_shape=(
            jax.ShapeDtypeStruct((T, heads * D), F32),
            jax.ShapeDtypeStruct((PK, 2 * D), BF),
            jax.ShapeDtypeStruct((T, 2 * D), BF),
        ),
        in_specs=[SM, VM, VM, VM, VM],
        out_specs=(VM, VM, VM),
        scratch_shapes=scratch,
        compiler_params=pltpu.CompilerParams(vmem_limit_bytes=61 * 2**20),
        name="attention_backward",
    )(answer_len, q, g, pkv, akv)


def reduce_kernel(
    hot_ref, dp_ref, da_ref, prompt_out, answer_out,
    blocks, parts, part_in, total, totals, mate, s1, r1, s2, r2, s3, r3, sm, rm,
):
    me = lax.axis_index("ctx")
    samp = lax.axis_index("samp")
    tp = lax.axis_index("tp")
    mine = samp * 2 + tp

    def member(i):
        other = lax.rem(mine + i, NG)
        return {"samp": other // 2, "tp": lax.rem(other, 2)}

    barrier = pltpu.get_barrier_semaphore()
    for i in range(1, NC):
        pl.semaphore_signal(
            barrier, inc=1, device_id={"ctx": lax.rem(me + i, NC)}, device_id_type=MESH
        )
    for i in range(1, NG):
        pl.semaphore_signal(barrier, inc=1, device_id=member(i), device_id_type=MESH)
    pl.semaphore_wait(barrier, NC - 1 + NG - 1)

    def block_copy(i):
        return pltpu.make_async_remote_copy(
            src_ref=dp_ref.at[lax.rem(me + i, NC)],
            dst_ref=blocks.at[i],
            send_sem=s1.at[i],
            recv_sem=r1.at[i],
            device_id={"ctx": lax.rem(me + i, NC)},
            device_id_type=MESH,
        )

    def part_copy(i):
        return pltpu.make_async_remote_copy(
            src_ref=parts.at[lax.rem(mine + i, NG)],
            dst_ref=part_in.at[i],
            send_sem=s2.at[i],
            recv_sem=r2.at[i],
            device_id=member(i),
            device_id_type=MESH,
        )

    def total_copy(i):
        return pltpu.make_async_remote_copy(
            src_ref=total,
            dst_ref=totals.at[mine],
            send_sem=s3.at[i],
            recv_sem=r3.at[i],
            device_id=member(i),
            device_id_type=MESH,
        )

    mate_copy = pltpu.make_async_remote_copy(
        src_ref=da_ref,
        dst_ref=mate,
        send_sem=sm,
        recv_sem=rm,
        device_id={"tp": 1 - tp},
        device_id_type=MESH,
    )
    for i in range(1, NC):
        block_copy(i).start()
    mate_copy.start()

    def add_block(block, weights, sums):
        block = block.astype(F32)
        return [s + block * weight_row(weights, p) for p, s in enumerate(sums)]

    acc = total.shape[0] // NP
    for i in range(1, NC):
        block_copy(i).wait_recv()
    for m in range(0, NG, 2):
        at = slice(m * acc, (m + 2) * acc)
        sums = [jnp.zeros((2 * acc, 2 * D), F32)] * NP
        sums = add_block(dp_ref[me, at, :], hot_ref[me], sums)
        for i in range(1, NC):
            sums = add_block(blocks[i, at, :], hot_ref[lax.rem(me - i + NC, NC)], sums)
        parts[m] = jnp.concatenate([s[:acc] for s in sums], axis=0).astype(BF)
        parts[m + 1] = jnp.concatenate([s[acc:] for s in sums], axis=0).astype(BF)
    for i in range(1, NG):
        part_copy(i).start()
    mate_copy.wait_recv()
    answer_out[...] = da_ref[...].astype(F32) + mate[...].astype(F32)
    whole = parts[mine].astype(F32)
    for i in range(1, NG):
        part_copy(i).wait_recv()
        whole = whole + part_in[i].astype(F32)
    total[...] = whole
    totals[mine] = whole
    for i in range(1, NG):
        total_copy(i).start()
    for i in range(1, NG):
        total_copy(i).wait_recv()
    for m in range(NG):
        for p in range(NP):
            prompt_out[p, m * acc : (m + 1) * acc, :] = totals[m, p * acc : (p + 1) * acc, :]
    mate_copy.wait_send()
    for i in range(1, NC):
        block_copy(i).wait_send()
    for i in range(1, NG):
        part_copy(i).wait_send()
        total_copy(i).wait_send()


def reduce(hot, dpkv, dakv):
    dma = pltpu.SemaphoreType.DMA
    part_rows = NP * BL // NG
    return pl.pallas_call(
        reduce_kernel,
        out_shape=(
            jax.ShapeDtypeStruct((NP, BL, 2 * D), F32),
            jax.ShapeDtypeStruct((T, 2 * D), F32),
        ),
        in_specs=[VM, VM, VM],
        out_specs=(VM, VM),
        scratch_shapes=[
            pltpu.VMEM((NC, BL, 2 * D), BF),
            pltpu.VMEM((NG, part_rows, 2 * D), BF),
            pltpu.VMEM((NG, part_rows, 2 * D), BF),
            pltpu.VMEM((part_rows, 2 * D), F32),
            pltpu.VMEM((NG, part_rows, 2 * D), F32),
            pltpu.VMEM((T, 2 * D), BF),
            dma((NC,)), dma((NC,)), dma((NG,)), dma((NG,)), dma((NG,)), dma((NG,)),
            dma, dma,
        ],
        compiler_params=pltpu.CompilerParams(collective_id=1, has_side_effects=True),
        name="reduce_grads",
    )(hot, dpkv.reshape(NC, BL, 2 * D), dakv)


def body(queries, out_grad, answer_kv, prompt_kv, answer_prompt, answer_len):
    chosen, hot = gather(answer_prompt, prompt_kv)
    dq, dpkv, dakv = compute(
        answer_len, queries[0], out_grad[0], chosen.reshape(PK, 2 * D), answer_kv[0]
    )
    prompt_grad, answer_grad = reduce(hot, dpkv, dakv)
    return dq[None], answer_grad[None], prompt_grad


def solution(mesh):
    placed = (
        P(("ctx", "samp"), None, "tp"),
        P(("ctx", "samp"), None, "tp"),
        P(("ctx", "samp"), None, None),
        P(None, "ctx", None),
        P(("ctx", "samp")),
        P(("ctx", "samp")),
    )
    return jax.shard_map(
        body,
        mesh=mesh,
        in_specs=placed,
        out_specs=(
            P(("ctx", "samp"), None, "tp"),
            P(("ctx", "samp"), None, None),
            P(None, "ctx", None),
        ),
        check_vma=False,
    )
```

time: 344 us -> 83.2 us (0.24); the launches traced: 339 us -> 82.7 us
  waiting for transfers between devices: 191 us -> 0 us
  Pallas kernels: 0 us -> 77.4 us
  matrix products: 71.3 us -> 0 us
  other arithmetic: 42.7 us -> 0 us
  local copies, waits for them, and re-layouts: 18.4 us -> 3.34 us
  between operations: 15.4 us -> 1.94 us
    psum x2 -> x0, waiting for transfers between devices: 91.9 us -> none  [the longest x1 70.6 us: body(): prompt_kv_grad = lax.psum(block_part, ('samp', 'tp'))]
    pallas_call x0 -> x3, Pallas kernels: none -> 77.4 us  [the longest x1 31.1 us: compute(): pl.pallas_call(functools.partial(compute_kernel, heads), out_shape=(jax.S...]
    dot_general x15 -> x0, matrix products: 71.3 us -> none  [the longest x3 31.3 us: block_terms(): jnp.einsum('athd,akd->athk', g_heads, kv_rows[:, :, head_width:], preferr...]
    reduce_scatter x1 -> x0, waiting for transfers between devices: 55 us -> none  [body(): lax.psum_scatter(grad_prompt_acc, 'ctx', scatter_dimension=1, tiled=True)]
    all_gather x1 -> x0, waiting for transfers between devices: 43.5 us -> none  [body(): whole_kv = lax.all_gather(prompt_kv, 'ctx', axis=1, tiled=True)]
    convert_element_type x2 -> x0, other arithmetic: 26.2 us -> none  [grad_terms(): dscores_b = (probs * (dprobs - row_delta[..., None])).astype(jnp.bfloat16)]
    unnamed x31 -> x2, local copies, waits for them, and re-layouts: 11.9 us -> 3.34 us
    another operation x4 -> x0, local copies, waits for them, and re-layouts: 6.49 us -> none
  transfers between devices with their start and end apart: 4 -> 0, of which waited for: 4 -> 0; matrix products, arithmetic and copies ran while one was open for 12% -> 0% of each run, Pallas kernels for 0% -> 0%
where the time goes in v1:
time: 83.2 us; the launch traced here: 82.7 us
  Pallas kernels  77.4 us (93%)
  local copies, waits for them, and re-layouts  3.34 us (4%)
  between operations  1.94 us (2%)
    pallas_call x1, Pallas kernels, compute(): pl.pallas_call(functools.partial(compute_kernel, heads), out_shape=(jax.S...  31.1 us
    pallas_call x1, Pallas kernels, reduce(): pl.pallas_call(reduce_kernel, out_shape=(jax.ShapeDtypeStruct((NP, BL, 2...  24.3 us
    pallas_call x1, Pallas kernels, gather(): pl.pallas_call(gather_kernel, out_shape=(jax.ShapeDtypeStruct((NC, BL, 2...  22 us
    unnamed x2, local copies, waits for them, and re-layouts  3.34 us

profile of v1, /device:TPU:1, one launch (start us, length us, event | category | flops | bytes accessed | tf_op | source)
XLA Modules:
  0.0 82.7 jit_solution(18156788558328523274)
XLA Ops:
  1.9 22.0 %gather_prompt.1 = (bf16[16,64,256]{2,1,0:T(8,128)(2,1)}, f32[16,8,128]{2,1,0:T(8,128)}) custom-call(s32[1]{0:T(128)S(6)} %copy.11.ap_ref, bf16[4,64,256]{2,1,0:T(8,128)(2,1)} %kv_ref.1), custom_call_target="tpu_custom_call" | custom-call | tf_op jit(solution)/shard_map/gather_prompt/pallas_call | solution.py:91
  24.0 31.1 %attention_backward.1 = (f32[256,3072]{1,0:T(8,128)}, bf16[1024,256]{1,0:T(8,128)(2,1)}, bf16[256,256]{1,0:T(8,128)(2,1)}) custom-call(s32[1]{0:T(128)S(6)} %copy.12.len_ref, bf16[256,3072]{1,0:T(8,128)(2,1)} %bitcast.7, bf16[256,3072]{1,0:T(8,128)(2,1)} %bitcast.8, bf16[1024,256]{1,0:T(8,128)(2,1)} %bitcast.10, bf16[256,256]{1,0:T(8,128)(2,1)} %bitcast.12), custom_call_target="tpu_custom_call" | custom-call | tf_op jit(solution)/shard_map/attention_backward/pallas_call | solution.py:205
  55.0 24.3 %reduce_grads.1 = (f32[4,64,256]{2,1,0:T(8,128)}, f32[256,256]{1,0:T(8,128)}) custom-call(f32[16,8,128]{2,1,0:T(8,128)} %get-tuple-element.12.hot_ref, bf16[16,64,256]{2,1,0:T(8,128)(2,1)} %bitcast.9, bf16[256,256]{1,0:T(8,128)(2,1)} %get-tuple-element.14.da_ref), custom_call_target="tpu_custom_call" | custom-call | tf_op jit(solution)/shard_map/reduce_grads/pallas_call | solution.py:327
  79.3 1.7 %copy.13 = f32[1,256,256]{2,1,0:T(8,128)} copy(f32[1,256,256]{2,1,0:T(8,128)} %bitcast.11) | data formatting | bytes 524288
  81.0 1.7 %copy.14 = f32[4,64,256]{2,1,0:T(8,128)} copy(f32[4,64,256]{2,1,0:T(8,128)} %get-tuple-element.22) | data formatting | bytes 524288
